TPU v7x, 128 devices: a whole 4x4x4 slice. The times are simulated.
128 devices in a mesh: depth: 8 (over y, core), tile: 16 (over x, z).
Axes of the slice: x: 4, y: 4, z: 4, core: 2. Of those that a mesh axis runs over, the one named last changes fastest.
Arguments:
- fields: float32 [2, 256, 256, 1024], P(None, 'depth', 'tile'), may hold values from -6 to 6
- colour_palette: float32 [3, 16], replicated, may hold values from 0.05 to 1
- opacity_palette: float32 [16], replicated, may hold values from 0.2 to 3
- tf_index: int32 [256], replicated, may hold values from 0 to 15
Outputs:
- image: float32 [4, 256, 1024], P(None, 'tile', 'depth')
All inputs are finite; a program needn't handle non-finite values.
Results may differ from a plain program's by a relative error of at most 0.0003.
Values sent between devices are 32-bit elements; how exact they have to be, the bound alone decides.
A program may use at most 64 MiB of HBM per device.

v0:
```python
import jax
import jax.numpy as jnp
import numpy as np
from jax import lax
from jax.sharding import PartitionSpec as P

taps_offset = np.arange(-4.0, 5.0)
gauss_bell = np.exp(-(taps_offset**2) / 8.0)
smooth_taps = tuple((float(weight) for weight in gauss_bell / np.sqrt(np.sum(gauss_bell**2))))
slope_raw = taps_offset * gauss_bell
slope_taps = tuple((float(weight) for weight in slope_raw / np.sqrt(np.sum(slope_raw**2))))


def extended(cells, sides, width):
    for axis, dim in sides:
        count = lax.axis_size(axis)
        ends = count - 1
        head = lax.slice_in_dim(cells, 0, width, axis=dim)
        tail = lax.slice_in_dim(cells, cells.shape[dim] - width, cells.shape[dim], axis=dim)
        cells = jnp.concatenate(
            [
                lax.ppermute(tail, axis, [(i, (i + 1) % count) for i in range(ends)]),
                cells,
                lax.ppermute(head, axis, [((i + 1) % count, i) for i in range(ends)]),
            ],
            axis=dim,
        )
    return cells


def filter_axis(field, taps, axis):
    count = field.shape[axis] - (len(taps) - 1)
    total = taps[0] * lax.slice_in_dim(field, 0, count, axis=axis)
    for offset in range(1, len(taps)):
        total = total + taps[offset] * lax.slice_in_dim(field, offset, offset + count, axis=axis)
    return total


def smooth_three(field, first):
    for axis in range(first, first + 3):
        field = filter_axis(field, smooth_taps, axis)
    return field


def slopes(smooth_a):
    core = smooth_a[4:-4, 4:-4, 4:-4]
    grad_z = filter_axis(smooth_a[:, 4:-4, 4:-4], slope_taps, 0)
    grad_x = filter_axis(smooth_a[4:-4, :, 4:-4], slope_taps, 1)
    grad_y = filter_axis(smooth_a[4:-4, 4:-4, :], slope_taps, 2)
    return (core, grad_z, grad_x, grad_y)


def shade_cells(smooth_a, smooth_b, grad_z, grad_x, grad_y, table, depth_total):
    bins = table.shape[1]
    slab_cells, strip_rows, column_count = smooth_a.shape
    level = (bins - 1) * jax.nn.sigmoid(1.5 * smooth_a)
    centres = jnp.arange(bins, dtype=jnp.float32)

    def one_plane(plane):
        flat = plane.reshape(1, strip_rows * column_count)
        hat_weights = jnp.maximum(0.0, 1.0 - jnp.abs(flat - centres[:, None]))
        mixed = jnp.dot(table, hat_weights, precision=lax.Precision.HIGHEST)
        return mixed.reshape(4, strip_rows, column_count)

    looked = jnp.moveaxis(lax.map(one_plane, level), 1, 0)
    facing = jnp.abs(0.26726 * grad_z + 0.53452 * grad_x + 0.80178 * grad_y)
    length = jnp.sqrt(jnp.maximum(grad_z * grad_z + grad_x * grad_x + grad_y * grad_y, 0.1))
    shade = 0.3 + 0.7 * facing / length
    optical = 1.5 * (2.0 / depth_total) * looked[3] * jax.nn.sigmoid(2.0 * smooth_b)
    depth_ids = jnp.arange(slab_cells, dtype=jnp.int32)
    strict_lower = (depth_ids[:, None] > depth_ids[None, :]).astype(jnp.float32)
    flat_optical = optical.reshape(slab_cells, strip_rows * column_count)
    before = jnp.dot(strict_lower, flat_optical, precision=lax.Precision.HIGHEST).reshape(
        optical.shape
    )
    ones_row = jnp.ones((1, slab_cells), jnp.float32)
    total = jnp.dot(ones_row, flat_optical, precision=lax.Precision.HIGHEST).reshape(
        strip_rows, column_count
    )
    weight = jnp.exp(-before) * -jnp.expm1(-optical)
    colour = jnp.sum(weight[None] * looked[:3] * shade[None], axis=1)
    return jnp.concatenate([colour, jnp.exp(-total)[None]], axis=0)


def blend_over(front, back):
    colour = front[:3] + front[3:4] * back[:3]
    return jnp.concatenate([colour, front[3:4] * back[3:4]], axis=0)


def local(fields, colour_palette, opacity_palette, tf_index):
    palette_size = colour_palette.shape[1]
    one_hot = (tf_index[None, :] == jnp.arange(palette_size, dtype=jnp.int32)[:, None]).astype(
        jnp.float32
    )
    table = jnp.concatenate(
        [
            jnp.dot(colour_palette, one_hot, precision=lax.Precision.HIGHEST),
            jnp.dot(opacity_palette[None], one_hot, precision=lax.Precision.HIGHEST),
        ],
        axis=0,
    )
    depth_count = lax.axis_size("depth")
    slab_cells = fields.shape[1]
    strip_rows = fields.shape[2]
    depth_total = slab_cells * depth_count
    wide_first = extended(fields[0], (("depth", 0), ("tile", 1)), 8)
    wide_first = jnp.pad(wide_first, ((0, 0), (0, 0), (8, 8)))
    wide_second = extended(fields[1], (("depth", 0), ("tile", 1)), 4)
    wide_second = jnp.pad(wide_second, ((0, 0), (0, 0), (4, 4)))
    smooth_a = smooth_three(wide_first, 0)
    smooth_b = smooth_three(wide_second, 0)
    depth_pos = (
        lax.axis_index("depth") * slab_cells - 4 + jnp.arange(slab_cells + 8, dtype=jnp.int32)
    )
    depth_ok = (depth_pos >= 0) & (depth_pos < depth_total)
    row_total = strip_rows * lax.axis_size("tile")
    row_pos = lax.axis_index("tile") * strip_rows - 4 + jnp.arange(strip_rows + 8, dtype=jnp.int32)
    row_ok = (row_pos >= 0) & (row_pos < row_total)
    column_count = fields.shape[3]
    column_pos = jnp.arange(column_count + 8, dtype=jnp.int32) - 4
    column_ok = (column_pos >= 0) & (column_pos < column_count)
    inside = depth_ok[:, None, None] & row_ok[None, :, None] & column_ok[None, None, :]
    smooth_a = jnp.where(inside, smooth_a, jnp.float32(0.0))
    core, grad_z, grad_x, grad_y = slopes(smooth_a)
    partial_value = shade_cells(core, smooth_b, grad_z, grad_x, grad_y, table, depth_total)
    rows, columns = (partial_value.shape[1], partial_value.shape[2])
    own_columns = columns // depth_count
    levels = depth_count.bit_length() - 1
    blocks = partial_value.reshape(4, rows, depth_count, own_columns)
    stack = lax.all_to_all(blocks, "depth", split_axis=2, concat_axis=2, tiled=True)
    for level_step in range(levels):
        stack = blend_over(stack[:, :, 0::2], stack[:, :, 1::2])
    return stack[:, :, 0]


def solution(mesh):
    placed = (P(None, "depth", "tile", None), P(), P(), P())
    return jax.shard_map(
        local, mesh=mesh, in_specs=placed, out_specs=P(None, "tile", "depth"), check_vma=False
    )
```

profile of v0, /device:TPU:7, one launch (start us, length us, event | category | flops | bytes accessed | tf_op | source)
XLA Modules:
  0.0 955.7 jit_solution(11518003850341516901)
XLA Ops:
  59.5 19.8 %collective-permute-done.2 = f32[48,8,1024]{2,0,1:T(8,128)S(1)} collective-permute-done((f32[48,8,1024]{2,0,1:T(8,128)}, f32[48,8,1024]{2,0,1:T(8,128)S(1)}, u32[]{:S(2)}, u32[]{:S(2)}) %collective-permute-start.2) | collective-permute-done | bytes 1572896 | tf_op jit(solution)/shard_map/ppermute | solution.py:22
  120.4 17.7 %multiply_add_fusion = f32[32,16,1024]{2,0,1:T(8,128)} fusion(f32[40,24,1032]{2,0,1:T(8,128)S(1)} %fusion.23), kind=kLoop, calls=%fused_computation.195 | loop fusion | flops 33554432 | bytes 54525952 | tf_op jit(solution)/shard_map/add | solution.py:68
  140.3 792.6 %while.11 = (s32[]{:T(128)}, f32[32,4,16,1024]{3,0,2,1:T(8,128)}, f32[32,16,1024]{2,0,1:T(8,128)}, f32[4,256]{1,0:T(4,128)S(1)}, s32[]{:T(128)}, /*index=5*/s32[]{:T(128)}) while((s32[]{:T(128)}, f32[32,4,16,1024]{3,0,2,1:T(8,128)}, f32[32,16,1024]{2,0,1:T(8,128)}, f32[4,256]{1,0:T(4,128)S(1)}, s32[]{:T(128)}, ...), condition=%wide.region_1.2_spmd.clone, body=%wide.region_0.1_spmd.clone.sunk | while | flops 218103808 | bytes 1511509 | solution.py:65
  141.4 17.2 %convolution_bitcast_fusion.3 = f32[4,16384]{1,0:T(4,128)S(1)} fusion(f32[4,256]{1,0:T(4,128)S(1)} %get-tuple-element.123, f32[16384]{0:T(1024)S(1)} %bitcast.94), kind=kOutput, calls=%fused_computation.1.clone.1 | convolution fusion | flops 218103808 | bytes 331776 | tf_op jit(solution)/shard_map/while/body/eval_jaxpr/dot_general | solution.py:62
  166.2 17.2 %convolution_bitcast_fusion.3 = f32[4,16384]{1,0:T(4,128)S(1)} fusion(f32[4,256]{1,0:T(4,128)S(1)} %get-tuple-element.123, f32[16384]{0:T(1024)S(1)} %bitcast.94), kind=kOutput, calls=%fused_computation.1.clone.1 | convolution fusion | flops 218103808 | bytes 331776 | tf_op jit(solution)/shard_map/while/body/eval_jaxpr/dot_general | solution.py:62
  191.0 17.2 %convolution_bitcast_fusion.3 = f32[4,16384]{1,0:T(4,128)S(1)} fusion(f32[4,256]{1,0:T(4,128)S(1)} %get-tuple-element.123, f32[16384]{0:T(1024)S(1)} %bitcast.94), kind=kOutput, calls=%fused_computation.1.clone.1 | convolution fusion | flops 218103808 | bytes 331776 | tf_op jit(solution)/shard_map/while/body/eval_jaxpr/dot_general | solution.py:62
  215.8 17.2 %convolution_bitcast_fusion.3 = f32[4,16384]{1,0:T(4,128)S(1)} fusion(f32[4,256]{1,0:T(4,128)S(1)} %get-tuple-element.123, f32[16384]{0:T(1024)S(1)} %bitcast.94), kind=kOutput, calls=%fused_computation.1.clone.1 | convolution fusion | flops 218103808 | bytes 331776 | tf_op jit(solution)/shard_map/while/body/eval_jaxpr/dot_general | solution.py:62
  240.6 17.2 %convolution_bitcast_fusion.3 = f32[4,16384]{1,0:T(4,128)S(1)} fusion(f32[4,256]{1,0:T(4,128)S(1)} %get-tuple-element.123, f32[16384]{0:T(1024)S(1)} %bitcast.94), kind=kOutput, calls=%fused_computation.1.clone.1 | convolution fusion | flops 218103808 | bytes 331776 | tf_op jit(solution)/shard_map/while/body/eval_jaxpr/dot_general | solution.py:62
  265.4 17.2 %convolution_bitcast_fusion.3 = f32[4,16384]{1,0:T(4,128)S(1)} fusion(f32[4,256]{1,0:T(4,128)S(1)} %get-tuple-element.123, f32[16384]{0:T(1024)S(1)} %bitcast.94), kind=kOutput, calls=%fused_computation.1.clone.1 | convolution fusion | flops 218103808 | bytes 331776 | tf_op jit(solution)/shard_map/while/body/eval_jaxpr/dot_general | solution.py:62
  339.8 17.2 %convolution_bitcast_fusion.3 = f32[4,16384]{1,0:T(4,128)S(1)} fusion(f32[4,256]{1,0:T(4,128)S(1)} %get-tuple-element.123, f32[16384]{0:T(1024)S(1)} %bitcast.94), kind=kOutput, calls=%fused_computation.1.clone.1 | convolution fusion | flops 218103808 | bytes 331776 | tf_op jit(solution)/shard_map/while/body/eval_jaxpr/dot_general | solution.py:62
  364.5 17.2 %convolution_bitcast_fusion.3 = f32[4,16384]{1,0:T(4,128)S(1)} fusion(f32[4,256]{1,0:T(4,128)S(1)} %get-tuple-element.123, f32[16384]{0:T(1024)S(1)} %bitcast.94), kind=kOutput, calls=%fused_computation.1.clone.1 | convolution fusion | flops 218103808 | bytes 331776 | tf_op jit(solution)/shard_map/while/body/eval_jaxpr/dot_general | solution.py:62
  389.3 17.2 %convolution_bitcast_fusion.3 = f32[4,16384]{1,0:T(4,128)S(1)} fusion(f32[4,256]{1,0:T(4,128)S(1)} %get-tuple-element.123, f32[16384]{0:T(1024)S(1)} %bitcast.94), kind=kOutput, calls=%fused_computation.1.clone.1 | convolution fusion | flops 218103808 | bytes 331776 | tf_op jit(solution)/shard_map/while/body/eval_jaxpr/dot_general | solution.py:62
  438.8 17.2 %convolution_bitcast_fusion.3 = f32[4,16384]{1,0:T(4,128)S(1)} fusion(f32[4,256]{1,0:T(4,128)S(1)} %get-tuple-element.123, f32[16384]{0:T(1024)S(1)} %bitcast.94), kind=kOutput, calls=%fused_computation.1.clone.1 | convolution fusion | flops 218103808 | bytes 331776 | tf_op jit(solution)/shard_map/while/body/eval_jaxpr/dot_general | solution.py:62
  463.6 17.2 %convolution_bitcast_fusion.3 = f32[4,16384]{1,0:T(4,128)S(1)} fusion(f32[4,256]{1,0:T(4,128)S(1)} %get-tuple-element.123, f32[16384]{0:T(1024)S(1)} %bitcast.94), kind=kOutput, calls=%fused_computation.1.clone.1 | convolution fusion | flops 218103808 | bytes 331776 | tf_op jit(solution)/shard_map/while/body/eval_jaxpr/dot_general | solution.py:62
  513.2 17.2 %convolution_bitcast_fusion.3 = f32[4,16384]{1,0:T(4,128)S(1)} fusion(f32[4,256]{1,0:T(4,128)S(1)} %get-tuple-element.123, f32[16384]{0:T(1024)S(1)} %bitcast.94), kind=kOutput, calls=%fused_computation.1.clone.1 | convolution fusion | flops 218103808 | bytes 331776 | tf_op jit(solution)/shard_map/while/body/eval_jaxpr/dot_general | solution.py:62
  537.9 17.2 %convolution_bitcast_fusion.3 = f32[4,16384]{1,0:T(4,128)S(1)} fusion(f32[4,256]{1,0:T(4,128)S(1)} %get-tuple-element.123, f32[16384]{0:T(1024)S(1)} %bitcast.94), kind=kOutput, calls=%fused_computation.1.clone.1 | convolution fusion | flops 218103808 | bytes 331776 | tf_op jit(solution)/shard_map/while/body/eval_jaxpr/dot_general | solution.py:62
  562.7 17.2 %convolution_bitcast_fusion.3 = f32[4,16384]{1,0:T(4,128)S(1)} fusion(f32[4,256]{1,0:T(4,128)S(1)} %get-tuple-element.123, f32[16384]{0:T(1024)S(1)} %bitcast.94), kind=kOutput, calls=%fused_computation.1.clone.1 | convolution fusion | flops 218103808 | bytes 331776 | tf_op jit(solution)/shard_map/while/body/eval_jaxpr/dot_general | solution.py:62
  587.5 17.2 %convolution_bitcast_fusion.3 = f32[4,16384]{1,0:T(4,128)S(1)} fusion(f32[4,256]{1,0:T(4,128)S(1)} %get-tuple-element.123, f32[16384]{0:T(1024)S(1)} %bitcast.94), kind=kOutput, calls=%fused_computation.1.clone.1 | convolution fusion | flops 218103808 | bytes 331776 | tf_op jit(solution)/shard_map/while/body/eval_jaxpr/dot_general | solution.py:62
  612.3 17.2 %convolution_bitcast_fusion.3 = f32[4,16384]{1,0:T(4,128)S(1)} fusion(f32[4,256]{1,0:T(4,128)S(1)} %get-tuple-element.123, f32[16384]{0:T(1024)S(1)} %bitcast.94), kind=kOutput, calls=%fused_computation.1.clone.1 | convolution fusion | flops 218103808 | bytes 331776 | tf_op jit(solution)/shard_map/while/body/eval_jaxpr/dot_general | solution.py:62
  637.0 17.2 %convolution_bitcast_fusion.3 = f32[4,16384]{1,0:T(4,128)S(1)} fusion(f32[4,256]{1,0:T(4,128)S(1)} %get-tuple-element.123, f32[16384]{0:T(1024)S(1)} %bitcast.94), kind=kOutput, calls=%fused_computation.1.clone.1 | convolution fusion | flops 218103808 | bytes 331776 | tf_op jit(solution)/shard_map/while/body/eval_jaxpr/dot_general | solution.py:62
  661.8 17.2 %convolution_bitcast_fusion.3 = f32[4,16384]{1,0:T(4,128)S(1)} fusion(f32[4,256]{1,0:T(4,128)S(1)} %get-tuple-element.123, f32[16384]{0:T(1024)S(1)} %bitcast.94), kind=kOutput, calls=%fused_computation.1.clone.1 | convolution fusion | flops 218103808 | bytes 331776 | tf_op jit(solution)/shard_map/while/body/eval_jaxpr/dot_general | solution.py:62
  686.6 17.2 %convolution_bitcast_fusion.3 = f32[4,16384]{1,0:T(4,128)S(1)} fusion(f32[4,256]{1,0:T(4,128)S(1)} %get-tuple-element.123, f32[16384]{0:T(1024)S(1)} %bitcast.94), kind=kOutput, calls=%fused_computation.1.clone.1 | convolution fusion | flops 218103808 | bytes 331776 | tf_op jit(solution)/shard_map/while/body/eval_jaxpr/dot_general | solution.py:62
  711.4 17.2 %convolution_bitcast_fusion.3 = f32[4,16384]{1,0:T(4,128)S(1)} fusion(f32[4,256]{1,0:T(4,128)S(1)} %get-tuple-element.123, f32[16384]{0:T(1024)S(1)} %bitcast.94), kind=kOutput, calls=%fused_computation.1.clone.1 | convolution fusion | flops 218103808 | bytes 331776 | tf_op jit(solution)/shard_map/while/body/eval_jaxpr/dot_general | solution.py:62
  736.2 17.2 %convolution_bitcast_fusion.3 = f32[4,16384]{1,0:T(4,128)S(1)} fusion(f32[4,256]{1,0:T(4,128)S(1)} %get-tuple-element.123, f32[16384]{0:T(1024)S(1)} %bitcast.94), kind=kOutput, calls=%fused_computation.1.clone.1 | convolution fusion | flops 218103808 | bytes 331776 | tf_op jit(solution)/shard_map/while/body/eval_jaxpr/dot_general | solution.py:62
  (190 shorter events, 556.7 us)
Async XLA Ops:
  0.0 20.1 %copy-start = (f32[3,16]{1,0:T(4,128)S(1)}, f32[3,16]{1,0:T(4,128)}, u32[]{:S(2)}) copy-start(f32[3,16]{1,0:T(4,128)} %param.7) | copy-start | bytes 580
  2.0 21.3 %collective-permute-start.5 = (f32[4,16,1024]{2,0,1:T(4,128)}, f32[4,16,1024]{2,0,1:T(4,128)S(1)}, u32[]{:S(2)}, u32[]{:S(2)}) collective-permute-start(f32[4,16,1024]{2,0,1:T(4,128)} %bitcast.80), channel_id=1, source_target_pairs={{16,0},{32,16},{48,32},{64,48},{80,64},{96,80},{112,96},{17,1},{33... | collective-permute-start | bytes 786440 | tf_op jit(solution)/shard_map/ppermute | solution.py:24
  4.5 13.2 %copy-start.6 = (f32[2,32,16,1024]{3,2,1,0:T(8,128)S(1)}, f32[2,32,16,1024]{3,2,1,0:T(8,128)}, u32[]{:S(2)}) copy-start(f32[2,32,16,1024]{3,2,1,0:T(8,128)} %param.6) | copy-start | bytes 12582916
  5.4 17.8 %collective-permute-start.4 = (f32[4,16,1024]{2,0,1:T(4,128)}, f32[4,16,1024]{2,0,1:T(4,128)}, u32[]{:S(2)}, u32[]{:S(2)}) collective-permute-start(f32[4,16,1024]{2,0,1:T(4,128)} %bitcast.81), channel_id=1, source_target_pairs={{0,16},{16,32},{32,48},{48,64},{64,80},{80,96},{96,112},{1,17},{17... | collective-permute-start | bytes 786440 | tf_op jit(solution)/shard_map/ppermute | solution.py:22
  11.1 25.1 %collective-permute-start.1 = (f32[8,16,1024]{2,0,1:T(8,128)}, f32[8,16,1024]{2,0,1:T(8,128)S(1)}, u32[]{:S(2)}, u32[]{:S(2)}) collective-permute-start(f32[8,16,1024]{2,0,1:T(8,128)} %bitcast.78), channel_id=1, source_target_pairs={{16,0},{32,16},{48,32},{64,48},{80,64},{96,80},{112,96},{17,1},{33... | collective-permute-start | bytes 1572872 | tf_op jit(solution)/shard_map/ppermute | solution.py:24
  14.1 22.0 %collective-permute-start = (f32[8,16,1024]{2,0,1:T(8,128)}, f32[8,16,1024]{2,0,1:T(8,128)S(1)}, u32[]{:S(2)}, u32[]{:S(2)}) collective-permute-start(f32[8,16,1024]{2,0,1:T(8,128)} %bitcast.79), channel_id=1, source_target_pairs={{0,16},{16,32},{32,48},{48,64},{64,80},{80,96},{96,112},{1,17},{17... | collective-permute-start | bytes 1572872 | tf_op jit(solution)/shard_map/ppermute | solution.py:22
  17.8 2.3 copy-start.8
  20.0 3.1 copy-start.9
  25.4 21.2 %collective-permute-start.6 = (f32[40,4,1024]{2,0,1:T(8,128)}, f32[40,4,1024]{2,0,1:T(8,128)}, u32[]{:S(2)}, u32[]{:S(2)}) collective-permute-start(f32[40,4,1024]{2,0,1:T(8,128)} %get-tuple-element.71), channel_id=1, source_target_pairs={{0,1},{1,2},{2,3},{3,4},{4,5},{5,6},{6,7},{7,8},{8,9},{9,10},{10,1... | collective-permute-start | bytes 1966088 | tf_op jit(solution)/shard_map/ppermute | solution.py:22
  29.0 19.1 %collective-permute-start.7 = (f32[40,4,1024]{2,0,1:T(8,128)}, f32[40,4,1024]{2,0,1:T(8,128)}, u32[]{:S(2)}, u32[]{:S(2)}) collective-permute-start(f32[40,4,1024]{2,0,1:T(8,128)} %get-tuple-element.72), channel_id=1, source_target_pairs={{1,0},{2,1},{3,2},{4,3},{5,4},{6,5},{7,6},{8,7},{9,8},{10,9},{11,1... | collective-permute-start | bytes 1966088 | tf_op jit(solution)/shard_map/ppermute | solution.py:24
  36.1 1.4 copy-start.2
  39.1 40.2 %collective-permute-start.2 = (f32[48,8,1024]{2,0,1:T(8,128)}, f32[48,8,1024]{2,0,1:T(8,128)S(1)}, u32[]{:S(2)}, u32[]{:S(2)}) collective-permute-start(f32[48,8,1024]{2,0,1:T(8,128)} %get-tuple-element.69), channel_id=1, source_target_pairs={{0,1},{1,2},{2,3},{3,4},{4,5},{5,6},{6,7},{7,8},{8,9},{9,10},{10,1... | collective-permute-start | bytes 4718600 | tf_op jit(solution)/shard_map/ppermute | solution.py:22
  41.0 40.0 %collective-permute-start.3 = (f32[48,8,1024]{2,0,1:T(8,128)S(1)}, f32[48,8,1024]{2,0,1:T(8,128)}, u32[]{:S(2)}, u32[]{:S(2)}) collective-permute-start(f32[48,8,1024]{2,0,1:T(8,128)S(1)} %get-tuple-element.70), channel_id=1, source_target_pairs={{1,0},{2,1},{3,2},{4,3},{5,4},{6,5},{7,6},{8,7},{9,8},{10,9},{11,1... | collective-permute-start | bytes 4718600 | tf_op jit(solution)/shard_map/ppermute | solution.py:24
  57.6 23.4 %copy-start.3 = (f32[1,32,16,1024]{3,1,2,0:T(8,128)S(1)}, f32[1,32,16,1024]{3,1,2,0:T(8,128)}, u32[]{:S(2)}) copy-start(f32[1,32,16,1024]{3,1,2,0:T(8,128)} %copy-done.2) | copy-start | bytes 6291460
  79.3 1.2 copy-start.7
  932.9 9.3 copy-start.4
  940.1 2.1 copy-start.5
  942.2 13.5 %copy-start.1 = (f32[3,16]{1,0:T(4,128)S(1)}, f32[3,16]{1,0:T(4,128)}, u32[]{:S(2)}) copy-start(f32[3,16]{1,0:T(4,128)} %param.7) | copy-start | bytes 580
where the time goes:
time: 964 us; the launch traced here: 956 us
  matrix products  553 us (57%)
  local copies, waits for them, and re-layouts  261 us (27%)
  other arithmetic  81.9 us (8%)
  starting transfers between devices  26.7 us (3%)
  waiting for transfers between devices  21.7 us (2%)
  blocking collectives  11 us (1%)
    dot_general x32, matrix products, one_plane(): mixed = jnp.dot(table, hat_weights, precision=lax.Precision.HIGHEST)  549 us
    dynamic_update_slice x32, local copies, waits for them, and re-layouts, shade_cells(): looked = jnp.moveaxis(lax.map(one_plane, level), 1, 0)  197 us
    dynamic_slice x32, local copies, waits for them, and re-layouts, shade_cells(): looked = jnp.moveaxis(lax.map(one_plane, level), 1, 0)  34.9 us
    add x4, other arithmetic, filter_axis(): total + taps[offset] * lax.slice_in_dim(field, offset, offset + count, ax...  29.2 us
    ppermute x4, waiting for transfers between devices, extended(): lax.ppermute(tail, axis, [(i, (i + 1) % count) for i in range(ends)])  19.8 us
  transfers between devices with their start and end apart: 8, of which 3 were waited for; matrix products, arithmetic and copies ran while one was open for 3% of the time, Pallas kernels for 0%

commit v1 on v0

v1 whole, which is shorter than its diff:
```python
import functools

import jax
import jax.numpy as jnp
import numpy as np
from jax import lax
from jax.experimental import pallas as pl
from jax.experimental.pallas import tpu as pltpu
from jax.sharding import PartitionSpec as P

MESH = pl.DeviceIdType.MESH
W = 128

offsets = np.arange(-4.0, 5.0)
bell = np.exp(-(offsets**2) / 8.0)
bell_norm = float(np.sqrt(np.sum(bell**2)))
slope_norm = float(np.sqrt(np.sum((offsets * bell) ** 2)))
RATIO = [float(np.exp(-(k * k) / 8.0)) for k in range(5)]
SMOOTH_SCALE = float(bell_norm**-3)
SLOPE = [0.0] + [float(k * RATIO[k] / RATIO[1]) for k in range(1, 5)]
SLOPE_SCALE = float(RATIO[1] / slope_norm)
LENGTH_FLOOR = float(0.1 / (SLOPE_SCALE * SMOOTH_SCALE) ** 2)


def even_sum(centre, pairs):
    total = centre
    for k in range(1, 5):
        low, high = pairs(k)
        total = total + RATIO[k] * (low + high)
    return total


def odd_sum(pairs):
    total = None
    for k in range(1, 5):
        low, high = pairs(k)
        term = high - low
        total = term if total is None else total + SLOPE[k] * term
    return total


def column_pairs(prev, cur, nxt):
    lane = lax.broadcasted_iota(jnp.int32, cur.shape, 1)

    def pairs(k):
        low = pltpu.roll(jnp.where(lane < W - k, cur, prev), k, 1)
        high = pltpu.roll(jnp.where(lane >= k, cur, nxt), W - k, 1)
        return low, high

    return pairs


def kernel(
    n_depth, n_tile, parts,
    fields, cpal, opal, tf, out,
    F0, F1, E0, X0, S, Y1, Z1, C, PT, R, tab, idx,
    load_sem, s_send, s_recv, f_send, f_recv,
):
    _, NZL, NXL, NYL = fields.shape
    NC = NYL // W
    d = lax.axis_index("depth")
    t = lax.axis_index("tile")
    d_up, d_dn = lax.rem(d + n_depth - 1, n_depth), lax.rem(d + 1, n_depth)
    t_up, t_dn = lax.rem(t + n_tile - 1, n_tile), lax.rem(t + 1, n_tile)
    comm = "comm" in parts

    def load(field, c):
        buf = (F0, F1)[field]
        return pltpu.make_async_copy(
            fields.at[field, :, :, c * W : (c + 1) * W], buf.at[c + 1], load_sem.at[field, c]
        )

    if comm:
        barrier = pltpu.get_barrier_semaphore()
        for where in ((d, t_up), (d, t_dn)):
            pl.semaphore_signal(barrier, inc=1, device_id=where, device_id_type=MESH)
        for step in range(1, n_depth):
            pl.semaphore_signal(
                barrier, inc=1, device_id=(lax.rem(d + step, n_depth), t), device_id_type=MESH
            )
    for field in range(2):
        for c in range(NC):
            load(field, c).start()

    zeros = jnp.zeros((8, W), jnp.float32)
    for j in range(4):
        tab[j] = zeros
    for j in range(3):
        tab[j, :, 0:16] = jnp.broadcast_to(cpal[j : j + 1, :], (8, 16))
    tab[3, :, 0:16] = jnp.broadcast_to(opal[...].reshape(1, 16), (8, 16))
    whole = tf[...].reshape(2, W)
    low_tf = jnp.broadcast_to(whole[0:1], (8, W))
    high_tf = jnp.broadcast_to(whole[1:2], (8, W))
    lane8 = lax.broadcasted_iota(jnp.int32, (8, W), 1)
    idx[0] = low_tf + 16 * pltpu.roll(jnp.where(lane8 >= 1, low_tf, high_tf), W - 1, 1)
    idx[1] = high_tf + 16 * pltpu.roll(high_tf, W - 1, 1)

    for buf in (F0, F1):
        buf[0] = jnp.zeros_like(buf[0])
        buf[NC + 1] = jnp.zeros_like(buf[NC + 1])
    S[0] = jnp.zeros_like(S[0])
    S[NC + 1] = jnp.zeros_like(S[NC + 1])

    if comm:
        pl.semaphore_wait(barrier, n_depth + 1)

    def remote(kind, side, c, src, dst, where):
        return pltpu.make_async_remote_copy(
            src_ref=src,
            dst_ref=dst,
            send_sem=s_send.at[kind, side, c],
            recv_sem=s_recv.at[kind, side, c],
            device_id=where,
            device_id_type=MESH,
        )

    def copies(kind, c):
        if kind == 0:
            return (
                remote(0, 0, c, E0.at[c, :, 16:24], E0.at[c, :, 0:8], (d, t_dn)),
                remote(0, 1, c, E0.at[c, :, 8:16], E0.at[c, :, 24:32], (d, t_up)),
            )
        if kind == 1:
            return (
                remote(1, 0, c, X0.at[c, 32:40], X0.at[c, 0:8], (d_dn, t)),
                remote(1, 1, c, X0.at[c, 8:16], X0.at[c, 40:48], (d_up, t)),
            )
        if kind == 2:
            return (
                remote(2, 0, c, Y1.at[c, 32:36], Y1.at[c, 0:4], (d_dn, t)),
                remote(2, 1, c, Y1.at[c, 4:8], Y1.at[c, 36:40], (d_up, t)),
            )
        return (
            remote(3, 0, c, Z1.at[c, :, 20:24], Z1.at[c, :, 4:8], (d, t_dn)),
            remote(3, 1, c, Z1.at[c, :, 8:12], Z1.at[c, :, 24:28], (d, t_up)),
        )

    def send(kind, c):
        if comm:
            for copy in copies(kind, c):
                copy.start()

    def receive(kind, c):
        if comm:
            for copy in copies(kind, c):
                copy.wait_recv()

    def final_copy(c, source, target):
        return pltpu.make_async_remote_copy(
            src_ref=PT.at[c],
            dst_ref=R.at[source],
            send_sem=f_send.at[c],
            recv_sem=f_recv.at[source],
            device_id=(target, t),
            device_id_type=MESH,
        )

    def clear(cond, ref, *where):
        @pl.when(cond)
        def _():
            part = ref.at[where]
            part[...] = jnp.zeros(part.shape, jnp.float32)

    def columns_smooth(buf, c, p):
        prev, cur, nxt = buf[c, p], buf[c + 1, p], buf[c + 2, p]
        return even_sum(cur, column_pairs(prev, cur, nxt))

    def stage_a0(c, _):
        @pl.when(c < NC - 1)
        def _():
            pltpu.make_async_copy(
                fields.at[0, :, :, 0:W], F0.at[c + 2], load_sem.at[0, c + 1]
            ).wait()

        def body(p, _):
            E0[c, p, 8:24] = columns_smooth(F0, c, p)
            return 0

        lax.fori_loop(0, NZL, body, 0, unroll=2)
        send(0, c)
        return 0

    def stage_a1(c, _):
        @pl.when(c < NC - 1)
        def _():
            pltpu.make_async_copy(
                fields.at[0, :, :, 0:W], F1.at[c + 2], load_sem.at[1, c + 1]
            ).wait()

        def body(p, _):
            Y1[c, p + 4] = columns_smooth(F1, c, p)
            return 0

        lax.fori_loop(0, NZL, body, 0, unroll=2)
        send(2, c)
        return 0

    def stage_b(c):
        receive(0, c)
        clear(t == 0, E0, c, slice(None), slice(0, 8))
        clear(t == n_tile - 1, E0, c, slice(None), slice(24, 32))

        def body(p, _):
            def pairs(k):
                return E0[c, p, 4 - k : 28 - k], E0[c, p, 4 + k : 28 + k]

            X0[c, p + 8] = even_sum(E0[c, p, 4:28], pairs)
            return 0

        lax.fori_loop(0, NZL, body, 0, unroll=2)
        clear(t == 0, X0, c, slice(8, 40), slice(0, 4))
        clear(t == n_tile - 1, X0, c, slice(8, 40), slice(20, 24))
        send(1, c)

    def stage_c(c):
        receive(1, c)
        clear(d == 0, X0, c, slice(0, 8))
        clear(d == n_depth - 1, X0, c, slice(40, 48))

        def body(g, _):
            for r in range(0, 24, 8):
                planes = [X0[c, g * 8 + i, r : r + 8] for i in range(16)]
                for i in range(8):
                    S[c + 1, g * 8 + i, r : r + 8] = even_sum(
                        planes[i + 4], lambda k: (planes[i + 4 - k], planes[i + 4 + k])
                    )
            return 0

        lax.fori_loop(0, (NZL + 8) // 8, body, 0)
        clear(d == 0, S, c + 1, slice(0, 4))
        clear(d == n_depth - 1, S, c + 1, slice(36, 40))

    def stage_b1(c):
        receive(2, c)
        clear(d == 0, Y1, c, slice(0, 4))
        clear(d == n_depth - 1, Y1, c, slice(36, 40))

        def body(g, _):
            for r in range(0, 16, 8):
                planes = [Y1[c, g * 8 + i, r : r + 8] for i in range(16)]
                for i in range(8):
                    Z1[c, g * 8 + i, r + 8 : r + 16] = even_sum(
                        planes[i + 4], lambda k: (planes[i + 4 - k], planes[i + 4 + k])
                    )
            return 0

        lax.fori_loop(0, NZL // 8, body, 0)
        send(3, c)

    def gather(table, where):
        return jnp.take_along_axis(table, where, axis=1, mode="promise_in_bounds")

    def stage_d(c):
        def body(p, _):
            for r in (0, 8):
                centre = S[c + 1, p + 4, r + 4 : r + 12]
                prev = S[c, p + 4, r + 4 : r + 12]
                nxt = S[c + 2, p + 4, r + 4 : r + 12]
                grad_z = odd_sum(
                    lambda k: (
                        S[c + 1, p + 4 - k, r + 4 : r + 12],
                        S[c + 1, p + 4 + k, r + 4 : r + 12],
                    )
                )
                grad_x = odd_sum(
                    lambda k: (
                        S[c + 1, p + 4, r + 4 - k : r + 12 - k],
                        S[c + 1, p + 4, r + 4 + k : r + 12 + k],
                    )
                )
                grad_y = odd_sum(column_pairs(prev, centre, nxt))
                facing = jnp.abs(0.26726 * grad_z + 0.53452 * grad_x + 0.80178 * grad_y)
                square = grad_z * grad_z + grad_x * grad_x + grad_y * grad_y
                shade = 0.3 + 0.7 * facing * lax.rsqrt(jnp.maximum(square, LENGTH_FLOOR))
                level = 127.5 + 127.5 * jnp.tanh((0.75 * SMOOTH_SCALE) * centre)
                bin_index = jnp.minimum(level.astype(jnp.int32), 254)
                fraction = level - bin_index.astype(jnp.float32)
                near = bin_index & 127
                pair = jnp.where(bin_index < 128, gather(idx[0], near), gather(idx[1], near))
                lower, upper = pair & 15, pair >> 4
                for j in range(4):
                    low = gather(tab[j], lower)
                    looked = low + (gather(tab[j], upper) - low) * fraction
                    C[c, j, p, r : r + 8] = looked if j == 3 else looked * shade
            return 0

        lax.fori_loop(0, NZL, body, 0)

    def stage_e(c, _):
        receive(3, c)
        clear(t == 0, Z1, c, slice(None), slice(4, 8))
        clear(t == n_tile - 1, Z1, c, slice(None), slice(24, 28))

        def body(p, carry):
            through, red, green, blue = carry

            def pairs(k):
                return Z1[c, p, 8 - k : 24 - k], Z1[c, p, 8 + k : 24 + k]

            smooth = even_sum(Z1[c, p, 8:24], pairs)
            gate = 0.5 + 0.5 * jnp.tanh(SMOOTH_SCALE * smooth)
            optical = (-1.5 * 2.0 / (NZL * n_depth)) * C[c, 3, p] * gate
            kept = through * jnp.exp(optical)
            weight = through - kept
            return (
                kept,
                red + weight * C[c, 0, p],
                green + weight * C[c, 1, p],
                blue + weight * C[c, 2, p],
            )

        none = jnp.zeros((NXL, W), jnp.float32)
        through, red, green, blue = lax.fori_loop(
            0, NZL, body, (jnp.ones((NXL, W), jnp.float32), none, none, none), unroll=2
        )

        def put(ref, where):
            for j, value in enumerate((red, green, blue, through)):
                ref[where, j] = value

        @pl.when(c == d)
        def _():
            put(R, d)

        @pl.when(c != d)
        def _():
            put(PT, c)
            if comm:
                final_copy(c, d, c).start()

        return 0

    load(0, 0).wait()
    if "a" in parts:
        lax.fori_loop(0, NC, stage_a0, 0)
    load(1, 0).wait()
    if "a" in parts:
        lax.fori_loop(0, NC, stage_a1, 0)
    else:
        for field in range(2):
            for c in range(1, NC):
                load(field, c).wait()

    def middle(i, _):
        @pl.when(i < NC)
        def _():
            if "b" in parts:
                stage_b(i)
            if "b1" in parts:
                stage_b1(i)

        @pl.when((i >= 1) & (i < NC + 1))
        def _():
            if "c" in parts:
                stage_c(i - 1)

        @pl.when(i >= 2)
        def _():
            if "d" in parts:
                stage_d(i - 2)

        return 0

    lax.fori_loop(0, NC + 2, middle, 0)
    if "e" in parts:
        lax.fori_loop(0, NC, stage_e, 0)

    if comm:

        def wait_final(i, _):
            @pl.when(i != d)
            def _():
                final_copy(i, i, i).wait_recv()

            return 0

        lax.fori_loop(0, n_depth, wait_final, 0)
    through, red, green, blue = R[0, 3], R[0, 0], R[0, 1], R[0, 2]
    for i in range(1, n_depth):
        red = red + through * R[i, 0]
        green = green + through * R[i, 1]
        blue = blue + through * R[i, 2]
        through = through * R[i, 3]
    for j, value in enumerate((red, green, blue, through)):
        out[j] = value

    if comm:

        def drain(c, _):
            for kind in range(4):
                for copy in copies(kind, c):
                    copy.wait_send()

            @pl.when(c != d)
            def _():
                final_copy(c, d, c).wait_send()

            return 0

        lax.fori_loop(0, NC, drain, 0)


ALL = ("comm", "a", "b", "b1", "c", "d", "e")


def local(n_depth, n_tile, parts, fields, colour_palette, opacity_palette, tf_index):
    _, planes, rows, columns = fields.shape
    chunks = columns // W
    f32 = jnp.float32
    vmem = pl.BlockSpec(memory_space=pltpu.VMEM)
    return pl.pallas_call(
        functools.partial(kernel, n_depth, n_tile, parts),
        out_shape=jax.ShapeDtypeStruct((4, rows, W), f32),
        in_specs=[pl.BlockSpec(memory_space=pl.ANY), vmem, vmem, vmem],
        out_specs=vmem,
        scratch_shapes=[
            pltpu.VMEM((chunks + 2, planes, rows, W), f32),
            pltpu.VMEM((chunks + 2, planes, rows, W), f32),
            pltpu.VMEM((chunks, planes, rows + 16, W), f32),
            pltpu.VMEM((chunks, planes + 16, rows + 8, W), f32),
            pltpu.VMEM((chunks + 2, planes + 8, rows + 8, W), f32),
            pltpu.VMEM((chunks, planes + 8, rows, W), f32),
            pltpu.VMEM((chunks, planes, rows + 16, W), f32),
            pltpu.VMEM((chunks, 4, planes, rows, W), f32),
            pltpu.VMEM((chunks, 4, rows, W), f32),
            pltpu.VMEM((chunks, 4, rows, W), f32),
            pltpu.VMEM((4, 8, W), f32),
            pltpu.VMEM((2, 8, W), jnp.int32),
            pltpu.SemaphoreType.DMA((2, chunks)),
            pltpu.SemaphoreType.DMA((4, 2, chunks)),
            pltpu.SemaphoreType.DMA((4, 2, chunks)),
            pltpu.SemaphoreType.DMA((chunks,)),
            pltpu.SemaphoreType.DMA((chunks,)),
        ],
        compiler_params=pltpu.CompilerParams(
            collective_id=0 if "comm" in parts else None,
            has_side_effects=True,
            vmem_limit_bytes=56 * 1024 * 1024,
        ),
    )(fields, colour_palette, opacity_palette, tf_index)


def solution(mesh, parts=ALL):
    placed = (P(None, "depth", "tile", None), P(), P(), P())
    return jax.shard_map(
        functools.partial(local, mesh.shape["depth"], mesh.shape["tile"], parts),
        mesh=mesh,
        in_specs=placed,
        out_specs=P(None, "tile", "depth"),
        check_vma=False,
    )
```

time: 964 us -> 106 us (0.11)
  the two profiles are of different devices: /device:TPU:7 before, /device:TPU:25 now
where the time goes in v1:
time: 106 us
  Pallas kernels  105 us (99%)
  local copies, waits for them, and re-layouts  1.38 us (1%)
    pallas_call x1, Pallas kernels, local(): pl.pallas_call(functools.partial(kernel, n_depth, n_tile, parts), out_sha...  105 us

profile of v1, /device:TPU:25, one launch (start us, length us, event | category | flops | bytes accessed | tf_op | source)
XLA Modules:
  0.0 106.3 jit_solution(787392190427984908)
XLA Ops:
  0.0 104.9 %shard_map.46 = f32[4,16,128]{2,1,0:T(8,128)} custom-call(f32[2,32,16,1024]{3,2,1,0:T(8,128)} %fields.1, f32[3,16]{1,0:T(4,128)} %cpal.1, f32[16]{0:T(128)} %opal.1, s32[256]{0:T(256)} %tf.1), custom_call_target="tpu_custom_call" | custom-call | tf_op jit(solution)/shard_map/pallas_call | solution.py:411
  104.9 1.4 %copy.6 = f32[4,16,128]{2,1,0:T(8,128)} copy(f32[4,16,128]{2,1,0:T(8,128)} %shard_map.46) | data formatting | bytes 65536

commit v2 on v1

--- a/solution.py
+++ b/solution.py
@@ -39,6 +39,36 @@
     return total
 
 
+def tap_matrices(taps, odd):
+    source = lax.broadcasted_iota(jnp.int32, (W, W), 0)
+    target = lax.broadcasted_iota(jnp.int32, (W, W), 1)
+    halves = []
+    for start in (source, jnp.where(source < 4, source + W, source - W)):
+        distance = start - target
+        matrix = jnp.zeros((W, W), jnp.float32)
+        for k in range(-4, 5):
+            tap = -taps[-k] if odd and k < 0 else taps[abs(k)]
+            matrix = jnp.where(distance == k, jnp.float32(tap), matrix)
+        if start is not source:
+            matrix = jnp.where((source < 4) | (source >= W - 4), matrix, 0.0)
+        high = matrix.astype(jnp.bfloat16)
+        low = (matrix - high.astype(jnp.float32)).astype(jnp.bfloat16)
+        halves += [high, high, low]
+    return jnp.concatenate(halves, axis=0)
+
+
+def column_filter(prev, cur, nxt, matrix):
+    lane = lax.broadcasted_iota(jnp.int32, cur.shape, 1)
+    pieces = []
+    for values in (cur, jnp.where(lane < 4, nxt, prev)):
+        high = values.astype(jnp.bfloat16)
+        low = (values - high.astype(jnp.float32)).astype(jnp.bfloat16)
+        pieces += [high, low, high]
+    return jnp.dot(
+        jnp.concatenate(pieces, axis=1), matrix, preferred_element_type=jnp.float32
+    )
+
+
 def column_pairs(prev, cur, nxt):
     lane = lax.broadcasted_iota(jnp.int32, cur.shape, 1)
 
@@ -53,7 +83,7 @@
 def kernel(
     n_depth, n_tile, parts,
     fields, cpal, opal, tf, out,
-    F0, F1, E0, X0, S, Y1, Z1, C, PT, R, tab, idx,
+    F0, F1, E0, X0, S, Y1, Z1, C, PT, R, tab, idx, taps,
     load_sem, s_send, s_recv, f_send, f_recv,
 ):
     _, NZL, NXL, NYL = fields.shape
@@ -82,19 +112,23 @@
         for c in range(NC):
             load(field, c).start()
 
-    zeros = jnp.zeros((8, W), jnp.float32)
+    entry = lax.broadcasted_iota(jnp.int32, (8, 16), 0)
+    column = lax.broadcasted_iota(jnp.int32, (8, 16), 1)
     for j in range(4):
-        tab[j] = zeros
-    for j in range(3):
-        tab[j, :, 0:16] = jnp.broadcast_to(cpal[j : j + 1, :], (8, 16))
-    tab[3, :, 0:16] = jnp.broadcast_to(opal[...].reshape(1, 16), (8, 16))
+        row = opal[...].reshape(1, 16) if j == 3 else cpal[j : j + 1, :]
+        for h in range(2):
+            picked = jnp.where(column == entry + 8 * h, jnp.broadcast_to(row, (8, 16)), 0.0)
+            tab[j, h] = jnp.broadcast_to(jnp.sum(picked, axis=1, keepdims=True), (8, W))
     whole = tf[...].reshape(2, W)
     low_tf = jnp.broadcast_to(whole[0:1], (8, W))
     high_tf = jnp.broadcast_to(whole[1:2], (8, W))
     lane8 = lax.broadcasted_iota(jnp.int32, (8, W), 1)
-    idx[0] = low_tf + 16 * pltpu.roll(jnp.where(lane8 >= 1, low_tf, high_tf), W - 1, 1)
-    idx[1] = high_tf + 16 * pltpu.roll(high_tf, W - 1, 1)
-
+    low_next = pltpu.roll(jnp.where(lane8 >= 1, low_tf, high_tf), W - 1, 1)
+    high_next = pltpu.roll(high_tf, W - 1, 1)
+    idx[...] = low_tf + 16 * low_next + 256 * high_tf + 4096 * high_next
+
+    taps[0] = tap_matrices(RATIO, False)
+    taps[1] = tap_matrices(SLOPE, True)
     for buf in (F0, F1):
         buf[0] = jnp.zeros_like(buf[0])
         buf[NC + 1] = jnp.zeros_like(buf[NC + 1])
@@ -161,9 +195,13 @@
             part = ref.at[where]
             part[...] = jnp.zeros(part.shape, jnp.float32)
 
+    MB = 16
+
     def columns_smooth(buf, c, p):
-        prev, cur, nxt = buf[c, p], buf[c + 1, p], buf[c + 2, p]
-        return even_sum(cur, column_pairs(prev, cur, nxt))
+        prev, cur, nxt = (
+            buf[c + i, pl.ds(p, MB)].reshape(MB * NXL, W) for i in range(3)
+        )
+        return column_filter(prev, cur, nxt, taps[0]).reshape(MB, NXL, W)
 
     def stage_a0(c, _):
         @pl.when(c < NC - 1)
@@ -173,10 +211,10 @@
             ).wait()
 
         def body(p, _):
-            E0[c, p, 8:24] = columns_smooth(F0, c, p)
-            return 0
-
-        lax.fori_loop(0, NZL, body, 0, unroll=2)
+            E0[c, pl.ds(p * MB, MB), 8:24] = columns_smooth(F0, c, p * MB)
+            return 0
+
+        lax.fori_loop(0, NZL // MB, body, 0)
         send(0, c)
         return 0
 
@@ -188,10 +226,10 @@
             ).wait()
 
         def body(p, _):
-            Y1[c, p + 4] = columns_smooth(F1, c, p)
-            return 0
-
-        lax.fori_loop(0, NZL, body, 0, unroll=2)
+            Y1[c, pl.ds(p * MB + 4, MB)] = columns_smooth(F1, c, p * MB)
+            return 0
+
+        lax.fori_loop(0, NZL // MB, body, 0)
         send(2, c)
         return 0
 
@@ -247,44 +285,72 @@
         lax.fori_loop(0, NZL // 8, body, 0)
         send(3, c)
 
-    def gather(table, where):
-        return jnp.take_along_axis(table, where, axis=1, mode="promise_in_bounds")
+    def gather(table, where, axis):
+        return jnp.take_along_axis(table, where, axis=axis, mode="promise_in_bounds")
+
+    G, UE = 8, 8
+    for part in parts:
+        if part[0] == "g":
+            G = int(part[1:])
+        if part[0] == "u":
+            UE = int(part[1:])
 
     def stage_d(c):
-        def body(p, _):
-            for r in (0, 8):
-                centre = S[c + 1, p + 4, r + 4 : r + 12]
-                prev = S[c, p + 4, r + 4 : r + 12]
-                nxt = S[c + 2, p + 4, r + 4 : r + 12]
-                grad_z = odd_sum(
-                    lambda k: (
-                        S[c + 1, p + 4 - k, r + 4 : r + 12],
-                        S[c + 1, p + 4 + k, r + 4 : r + 12],
-                    )
+        def slope(p, _):
+            prev, cur, nxt = (
+                S[c + i, pl.ds(p * MB + 4, MB), 4:20].reshape(MB * NXL, W) for i in range(3)
+            )
+            C[c, 0, pl.ds(p * MB, MB)] = column_filter(prev, cur, nxt, taps[1]).reshape(MB, NXL, W)
+            return 0
+
+        lax.fori_loop(0, NZL // MB, slope, 0)
+
+        def cells(p, r):
+            centre = S[c + 1, p + 4, r + 4 : r + 12]
+            grad_z = odd_sum(
+                lambda k: (
+                    S[c + 1, p + 4 - k, r + 4 : r + 12],
+                    S[c + 1, p + 4 + k, r + 4 : r + 12],
                 )
-                grad_x = odd_sum(
-                    lambda k: (
-                        S[c + 1, p + 4, r + 4 - k : r + 12 - k],
-                        S[c + 1, p + 4, r + 4 + k : r + 12 + k],
-                    )
+            )
+            grad_x = odd_sum(
+                lambda k: (
+                    S[c + 1, p + 4, r + 4 - k : r + 12 - k],
+                    S[c + 1, p + 4, r + 4 + k : r + 12 + k],
                 )
-                grad_y = odd_sum(column_pairs(prev, centre, nxt))
-                facing = jnp.abs(0.26726 * grad_z + 0.53452 * grad_x + 0.80178 * grad_y)
-                square = grad_z * grad_z + grad_x * grad_x + grad_y * grad_y
-                shade = 0.3 + 0.7 * facing * lax.rsqrt(jnp.maximum(square, LENGTH_FLOOR))
-                level = 127.5 + 127.5 * jnp.tanh((0.75 * SMOOTH_SCALE) * centre)
-                bin_index = jnp.minimum(level.astype(jnp.int32), 254)
-                fraction = level - bin_index.astype(jnp.float32)
-                near = bin_index & 127
-                pair = jnp.where(bin_index < 128, gather(idx[0], near), gather(idx[1], near))
-                lower, upper = pair & 15, pair >> 4
+            )
+            grad_y = C[c, 0, p, r : r + 8]
+            facing = jnp.abs(0.26726 * grad_z + 0.53452 * grad_x + 0.80178 * grad_y)
+            square = grad_z * grad_z + grad_x * grad_x + grad_y * grad_y
+            shade = 0.3 + 0.7 * facing * lax.rsqrt(jnp.maximum(square, LENGTH_FLOOR))
+            level = 127.5 + 127.5 * jnp.tanh((0.75 * SMOOTH_SCALE) * centre)
+            bin_index = jnp.minimum(level.astype(jnp.int32), 254)
+            fraction = level - bin_index.astype(jnp.float32)
+            if "ng" in parts:
+                return [fraction, shade, level, shade]
+            pair = gather(idx[...], bin_index & 127, 1) >> ((bin_index >> 7) * 8)
+            lower, upper = pair & 15, (pair >> 4) & 15
+            lower_row, upper_row = lower & 7, upper & 7
+            lower_half, upper_half = lower < 8, upper < 8
+            found = []
+            for j in range(4):
+                halves = [tab[j, h] for h in range(2)]
+                low, high = (
+                    jnp.where(half, gather(halves[0], row, 0), gather(halves[1], row, 0))
+                    for half, row in ((lower_half, lower_row), (upper_half, upper_row))
+                )
+                looked = low + (high - low) * fraction
+                found.append(looked if j == 3 else looked * shade)
+            return found
+
+        def body(g, _):
+            places = [(g * G + i, r) for i in range(G) for r in (0, 8)]
+            for (p, r), found in zip(places, [cells(*place) for place in places]):
                 for j in range(4):
-                    low = gather(tab[j], lower)
-                    looked = low + (gather(tab[j], upper) - low) * fraction
-                    C[c, j, p, r : r + 8] = looked if j == 3 else looked * shade
-            return 0
-
-        lax.fori_loop(0, NZL, body, 0)
+                    C[c, j, p, r : r + 8] = found[j]
+            return 0
+
+        lax.fori_loop(0, NZL // G, body, 0)
 
     def stage_e(c, _):
         receive(3, c)
@@ -311,7 +377,7 @@
 
         none = jnp.zeros((NXL, W), jnp.float32)
         through, red, green, blue = lax.fori_loop(
-            0, NZL, body, (jnp.ones((NXL, W), jnp.float32), none, none, none), unroll=2
+            0, NZL, body, (jnp.ones((NXL, W), jnp.float32), none, none, none), unroll=UE
         )
 
         def put(ref, where):
@@ -424,8 +490,9 @@
             pltpu.VMEM((chunks, 4, planes, rows, W), f32),
             pltpu.VMEM((chunks, 4, rows, W), f32),
             pltpu.VMEM((chunks, 4, rows, W), f32),
-            pltpu.VMEM((4, 8, W), f32),
-            pltpu.VMEM((2, 8, W), jnp.int32),
+            pltpu.VMEM((4, 2, 8, W), f32),
+            pltpu.VMEM((8, W), jnp.int32),
+            pltpu.VMEM((2, 6 * W, W), jnp.bfloat16),
             pltpu.SemaphoreType.DMA((2, chunks)),
             pltpu.SemaphoreType.DMA((4, 2, chunks)),
             pltpu.SemaphoreType.DMA((4, 2, chunks)),

time: 106 us -> 52.2 us (0.49)
  Pallas kernels: 105 us -> 50.7 us
    pallas_call x1, Pallas kernels: 105 us -> 50.7 us  [local(): pl.pallas_call(functools.partial(kernel, n_depth, n_tile, parts), out_sha...]
where the time goes in v2:
time: 52.2 us; the launch traced here: 52 us
  Pallas kernels  50.7 us (97%)
  local copies, waits for them, and re-layouts  1.38 us (3%)
    pallas_call x1, Pallas kernels, local(): pl.pallas_call(functools.partial(kernel, n_depth, n_tile, parts), out_sha...  50.7 us
    unnamed x1, local copies, waits for them, and re-layouts  1.38 us

profile of v2, /device:TPU:25, one launch (start us, length us, event | category | flops | bytes accessed | tf_op | source)
XLA Modules:
  0.0 52.0 jit_solution(5011240929012556285)
XLA Ops:
  0.0 50.7 %shard_map.46 = f32[4,16,128]{2,1,0:T(8,128)} custom-call(f32[2,32,16,1024]{3,2,1,0:T(8,128)} %fields.1, f32[3,16]{1,0:T(4,128)} %cpal.1, f32[16]{0:T(128)} %opal.1, s32[256]{0:T(256)} %tf.1), custom_call_target="tpu_custom_call" | custom-call | tf_op jit(solution)/shard_map/pallas_call | solution.py:477
  50.7 1.4 %copy.6 = f32[4,16,128]{2,1,0:T(8,128)} copy(f32[4,16,128]{2,1,0:T(8,128)} %shard_map.46) | data formatting | bytes 65536

commit v3 on v2

--- a/solution.py
+++ b/solution.py
@@ -10,6 +10,7 @@
 
 MESH = pl.DeviceIdType.MESH
 W = 128
+THIRD = {5: (0, 1), 6: (2, 3, 4), 7: (5, 6, 7)}
 
 offsets = np.arange(-4.0, 5.0)
 bell = np.exp(-(offsets**2) / 8.0)
@@ -69,22 +70,11 @@
     )
 
 
-def column_pairs(prev, cur, nxt):
-    lane = lax.broadcasted_iota(jnp.int32, cur.shape, 1)
-
-    def pairs(k):
-        low = pltpu.roll(jnp.where(lane < W - k, cur, prev), k, 1)
-        high = pltpu.roll(jnp.where(lane >= k, cur, nxt), W - k, 1)
-        return low, high
-
-    return pairs
-
-
 def kernel(
-    n_depth, n_tile, parts,
-    fields, cpal, opal, tf, out,
-    F0, F1, E0, X0, S, Y1, Z1, C, PT, R, tab, idx, taps,
-    load_sem, s_send, s_recv, f_send, f_recv,
+    n_depth, n_tile,
+    fields, colour, opacity, entries, out,
+    F0, F1, E0, X0, S, Y1, Z1, C, PT, R, tab, idx, taps, cpal, opal, tf,
+    load_sem, table_sem, s_send, s_recv, f_send, f_recv,
 ):
     _, NZL, NXL, NYL = fields.shape
     NC = NYL // W
@@ -92,7 +82,6 @@
     t = lax.axis_index("tile")
     d_up, d_dn = lax.rem(d + n_depth - 1, n_depth), lax.rem(d + 1, n_depth)
     t_up, t_dn = lax.rem(t + n_tile - 1, n_tile), lax.rem(t + 1, n_tile)
-    comm = "comm" in parts
 
     def load(field, c):
         buf = (F0, F1)[field]
@@ -100,43 +89,46 @@
             fields.at[field, :, :, c * W : (c + 1) * W], buf.at[c + 1], load_sem.at[field, c]
         )
 
-    if comm:
-        barrier = pltpu.get_barrier_semaphore()
-        for where in ((d, t_up), (d, t_dn)):
+    barrier = pltpu.get_barrier_semaphore()
+    beside = ((t > 0, (d, t_up)), (t < n_tile - 1, (d, t_dn)))
+    for present, where in beside:
+
+        @pl.when(present)
+        def _():
             pl.semaphore_signal(barrier, inc=1, device_id=where, device_id_type=MESH)
-        for step in range(1, n_depth):
-            pl.semaphore_signal(
-                barrier, inc=1, device_id=(lax.rem(d + step, n_depth), t), device_id_type=MESH
-            )
+
+    for step in range(1, n_depth):
+        pl.semaphore_signal(
+            barrier, inc=1, device_id=(lax.rem(d + step, n_depth), t), device_id_type=MESH
+        )
     for field in range(2):
         for c in range(NC):
             load(field, c).start()
 
-    entry = lax.broadcasted_iota(jnp.int32, (8, 16), 0)
-    column = lax.broadcasted_iota(jnp.int32, (8, 16), 1)
-    for j in range(4):
-        row = opal[...].reshape(1, 16) if j == 3 else cpal[j : j + 1, :]
-        for h in range(2):
-            picked = jnp.where(column == entry + 8 * h, jnp.broadcast_to(row, (8, 16)), 0.0)
-            tab[j, h] = jnp.broadcast_to(jnp.sum(picked, axis=1, keepdims=True), (8, W))
-    whole = tf[...].reshape(2, W)
-    low_tf = jnp.broadcast_to(whole[0:1], (8, W))
-    high_tf = jnp.broadcast_to(whole[1:2], (8, W))
-    lane8 = lax.broadcasted_iota(jnp.int32, (8, W), 1)
-    low_next = pltpu.roll(jnp.where(lane8 >= 1, low_tf, high_tf), W - 1, 1)
-    high_next = pltpu.roll(high_tf, W - 1, 1)
-    idx[...] = low_tf + 16 * low_next + 256 * high_tf + 4096 * high_next
-
-    taps[0] = tap_matrices(RATIO, False)
-    taps[1] = tap_matrices(SLOPE, True)
-    for buf in (F0, F1):
-        buf[0] = jnp.zeros_like(buf[0])
-        buf[NC + 1] = jnp.zeros_like(buf[NC + 1])
-    S[0] = jnp.zeros_like(S[0])
-    S[NC + 1] = jnp.zeros_like(S[NC + 1])
-
-    if comm:
-        pl.semaphore_wait(barrier, n_depth + 1)
+    small = [
+        pltpu.make_async_copy(source, target, table_sem.at[i])
+        for i, (source, target) in enumerate(((colour, cpal), (opacity, opal), (entries, tf)))
+    ]
+    for copy in small:
+        copy.start()
+
+    def tables():
+        for copy in small:
+            copy.wait()
+        entry = lax.broadcasted_iota(jnp.int32, (8, 16), 0)
+        column = lax.broadcasted_iota(jnp.int32, (8, 16), 1)
+        for j in range(4):
+            row = opal[...].reshape(1, 16) if j == 3 else cpal[j : j + 1, :]
+            for h in range(2):
+                picked = jnp.where(column == entry + 8 * h, jnp.broadcast_to(row, (8, 16)), 0.0)
+                tab[j, h] = jnp.broadcast_to(jnp.sum(picked, axis=1, keepdims=True), (8, W))
+        whole = tf[...].reshape(2, W)
+        low_tf = jnp.broadcast_to(whole[0:1], (8, W))
+        high_tf = jnp.broadcast_to(whole[1:2], (8, W))
+        lane8 = lax.broadcasted_iota(jnp.int32, (8, W), 1)
+        low_next = pltpu.roll(jnp.where(lane8 >= 1, low_tf, high_tf), W - 1, 1)
+        high_next = pltpu.roll(high_tf, W - 1, 1)
+        idx[...] = low_tf + 16 * low_next + 256 * high_tf + 4096 * high_next
 
     def remote(kind, side, c, src, dst, where):
         return pltpu.make_async_remote_copy(
@@ -169,15 +161,19 @@
             remote(3, 1, c, Z1.at[c, :, 8:12], Z1.at[c, :, 24:28], (d, t_up)),
         )
 
+    def each_present(kind, c, act, incoming=False):
+        up, down = (d > 0, d < n_depth - 1) if kind in (1, 2) else (t > 0, t < n_tile - 1)
+        for present, copy in zip((up, down) if incoming else (down, up), copies(kind, c)):
+
+            @pl.when(present)
+            def _():
+                act(copy)
+
     def send(kind, c):
-        if comm:
-            for copy in copies(kind, c):
-                copy.start()
+        each_present(kind, c, lambda copy: copy.start())
 
     def receive(kind, c):
-        if comm:
-            for copy in copies(kind, c):
-                copy.wait_recv()
+        each_present(kind, c, lambda copy: copy.wait_recv(), incoming=True)
 
     def final_copy(c, source, target):
         return pltpu.make_async_remote_copy(
@@ -203,35 +199,30 @@
         )
         return column_filter(prev, cur, nxt, taps[0]).reshape(MB, NXL, W)
 
-    def stage_a0(c, _):
+    def load_next(field, c):
         @pl.when(c < NC - 1)
         def _():
             pltpu.make_async_copy(
-                fields.at[0, :, :, 0:W], F0.at[c + 2], load_sem.at[0, c + 1]
+                fields.at[0, :, :, 0:W], (F0, F1)[field].at[c + 2], load_sem.at[field, c + 1]
             ).wait()
+
+    def stage_a0(c):
+        load_next(0, c)
 
         def body(p, _):
             E0[c, pl.ds(p * MB, MB), 8:24] = columns_smooth(F0, c, p * MB)
             return 0
 
         lax.fori_loop(0, NZL // MB, body, 0)
-        send(0, c)
-        return 0
-
-    def stage_a1(c, _):
-        @pl.when(c < NC - 1)
-        def _():
-            pltpu.make_async_copy(
-                fields.at[0, :, :, 0:W], F1.at[c + 2], load_sem.at[1, c + 1]
-            ).wait()
+
+    def stage_a1(c):
+        load_next(1, c)
 
         def body(p, _):
             Y1[c, pl.ds(p * MB + 4, MB)] = columns_smooth(F1, c, p * MB)
             return 0
 
         lax.fori_loop(0, NZL // MB, body, 0)
-        send(2, c)
-        return 0
 
     def stage_b(c):
         receive(0, c)
@@ -283,17 +274,11 @@
             return 0
 
         lax.fori_loop(0, NZL // 8, body, 0)
-        send(3, c)
 
     def gather(table, where, axis):
         return jnp.take_along_axis(table, where, axis=axis, mode="promise_in_bounds")
 
     G, UE = 8, 8
-    for part in parts:
-        if part[0] == "g":
-            G = int(part[1:])
-        if part[0] == "u":
-            UE = int(part[1:])
 
     def stage_d(c):
         def slope(p, _):
@@ -326,8 +311,6 @@
             level = 127.5 + 127.5 * jnp.tanh((0.75 * SMOOTH_SCALE) * centre)
             bin_index = jnp.minimum(level.astype(jnp.int32), 254)
             fraction = level - bin_index.astype(jnp.float32)
-            if "ng" in parts:
-                return [fraction, shade, level, shade]
             pair = gather(idx[...], bin_index & 127, 1) >> ((bin_index >> 7) * 8)
             lower, upper = pair & 15, (pair >> 4) & 15
             lower_row, upper_row = lower & 7, upper & 7
@@ -352,7 +335,7 @@
 
         lax.fori_loop(0, NZL // G, body, 0)
 
-    def stage_e(c, _):
+    def stage_e(c):
         receive(3, c)
         clear(t == 0, Z1, c, slice(None), slice(4, 8))
         clear(t == n_tile - 1, Z1, c, slice(None), slice(24, 28))
@@ -391,56 +374,84 @@
         @pl.when(c != d)
         def _():
             put(PT, c)
-            if comm:
-                final_copy(c, d, c).start()
-
-        return 0
-
+            final_copy(c, d, c).start()
+
+    def every(stage, start=0):
+        def step(c, _):
+            stage(c)
+            return 0
+
+        lax.fori_loop(start, NC, step, 0)
+
+    taps[0] = tap_matrices(RATIO, False)
+    for buf in (F0, F1):
+        buf[0] = jnp.zeros_like(buf[0])
+        buf[NC + 1] = jnp.zeros_like(buf[NC + 1])
     load(0, 0).wait()
-    if "a" in parts:
-        lax.fori_loop(0, NC, stage_a0, 0)
+    stage_a0(0)
+    pl.semaphore_wait(
+        barrier, n_depth - 1 + (t > 0).astype(jnp.int32) + (t < n_tile - 1).astype(jnp.int32)
+    )
+    send(0, 0)
+
+    def first_field(c):
+        stage_a0(c)
+        send(0, c)
+
+    every(first_field, 1)
     load(1, 0).wait()
-    if "a" in parts:
-        lax.fori_loop(0, NC, stage_a1, 0)
-    else:
-        for field in range(2):
-            for c in range(1, NC):
-                load(field, c).wait()
+
+    def second_field(c):
+        stage_a1(c)
+        send(2, c)
+
+    every(second_field)
+    tables()
+    taps[1] = tap_matrices(SLOPE, True)
+    S[0] = jnp.zeros_like(S[0])
+    S[NC + 1] = jnp.zeros_like(S[NC + 1])
+    every(stage_b1)
+
+    def in_turn(j):
+        return lax.rem(d + 1 + j, NC)
 
     def middle(i, _):
         @pl.when(i < NC)
         def _():
-            if "b" in parts:
-                stage_b(i)
-            if "b1" in parts:
-                stage_b1(i)
+            stage_b(i)
+
+        for step, turns in THIRD.items():
+
+            @pl.when(i == step)
+            def _():
+                for j in turns:
+                    send(3, in_turn(j))
 
         @pl.when((i >= 1) & (i < NC + 1))
         def _():
-            if "c" in parts:
-                stage_c(i - 1)
+            stage_c(i - 1)
 
         @pl.when(i >= 2)
         def _():
-            if "d" in parts:
-                stage_d(i - 2)
+            stage_d(i - 2)
 
         return 0
 
     lax.fori_loop(0, NC + 2, middle, 0)
-    if "e" in parts:
-        lax.fori_loop(0, NC, stage_e, 0)
-
-    if comm:
-
-        def wait_final(i, _):
-            @pl.when(i != d)
-            def _():
-                final_copy(i, i, i).wait_recv()
-
-            return 0
-
-        lax.fori_loop(0, n_depth, wait_final, 0)
+
+    def last(j):
+        stage_e(in_turn(j))
+
+    every(last)
+
+    def wait_final(i, _):
+        @pl.when(i != d)
+        def _():
+            final_copy(i, i, i).wait_recv()
+
+        return 0
+
+    lax.fori_loop(0, n_depth, wait_final, 0)
     through, red, green, blue = R[0, 3], R[0, 0], R[0, 1], R[0, 2]
     for i in range(1, n_depth):
         red = red + through * R[i, 0]
@@ -450,34 +461,28 @@
     for j, value in enumerate((red, green, blue, through)):
         out[j] = value
 
-    if comm:
-
-        def drain(c, _):
-            for kind in range(4):
-                for copy in copies(kind, c):
-                    copy.wait_send()
-
-            @pl.when(c != d)
-            def _():
-                final_copy(c, d, c).wait_send()
-
-            return 0
-
-        lax.fori_loop(0, NC, drain, 0)
-
-
-ALL = ("comm", "a", "b", "b1", "c", "d", "e")
-
-
-def local(n_depth, n_tile, parts, fields, colour_palette, opacity_palette, tf_index):
+    def drain(c, _):
+        for kind in range(4):
+            each_present(kind, c, lambda copy: copy.wait_send())
+
+        @pl.when(c != d)
+        def _():
+            final_copy(c, d, c).wait_send()
+
+        return 0
+
+    lax.fori_loop(0, NC, drain, 0)
+
+
+def local(n_depth, n_tile, fields, colour_palette, opacity_palette, tf_index):
     _, planes, rows, columns = fields.shape
     chunks = columns // W
     f32 = jnp.float32
     vmem = pl.BlockSpec(memory_space=pltpu.VMEM)
     return pl.pallas_call(
-        functools.partial(kernel, n_depth, n_tile, parts),
-        out_shape=jax.ShapeDtypeStruct((4, rows, W), f32),
-        in_specs=[pl.BlockSpec(memory_space=pl.ANY), vmem, vmem, vmem],
+        functools.partial(kernel, n_depth, n_tile),
+        out_shape=pltpu.VMEM((4, rows, W), f32),
+        in_specs=[pl.BlockSpec(memory_space=pl.ANY)] * 4,
         out_specs=vmem,
         scratch_shapes=[
             pltpu.VMEM((chunks + 2, planes, rows, W), f32),
@@ -493,24 +498,28 @@
             pltpu.VMEM((4, 2, 8, W), f32),
             pltpu.VMEM((8, W), jnp.int32),
             pltpu.VMEM((2, 6 * W, W), jnp.bfloat16),
+            pltpu.VMEM(colour_palette.shape, f32),
+            pltpu.VMEM(opacity_palette.shape, f32),
+            pltpu.VMEM(tf_index.shape, jnp.int32),
             pltpu.SemaphoreType.DMA((2, chunks)),
+            pltpu.SemaphoreType.DMA((3,)),
             pltpu.SemaphoreType.DMA((4, 2, chunks)),
             pltpu.SemaphoreType.DMA((4, 2, chunks)),
             pltpu.SemaphoreType.DMA((chunks,)),
             pltpu.SemaphoreType.DMA((chunks,)),
         ],
         compiler_params=pltpu.CompilerParams(
-            collective_id=0 if "comm" in parts else None,
+            collective_id=0,
             has_side_effects=True,
             vmem_limit_bytes=56 * 1024 * 1024,
         ),
     )(fields, colour_palette, opacity_palette, tf_index)
 
 
-def solution(mesh, parts=ALL):
+def solution(mesh):
     placed = (P(None, "depth", "tile", None), P(), P(), P())
     return jax.shard_map(
-        functools.partial(local, mesh.shape["depth"], mesh.shape["tile"], parts),
+        functools.partial(local, mesh.shape["depth"], mesh.shape["tile"]),
         mesh=mesh,
         in_specs=placed,
         out_specs=P(None, "tile", "depth"),

time: 52.2 us -> 48.6 us (0.931)
  the two profiles are of different devices: /device:TPU:25 before, /device:TPU:7 now
where the time goes in v3:
time: 48.6 us; the launch traced here: 48.5 us
  Pallas kernels  47.9 us (99%)
  local copies, waits for them, and re-layouts  0.62 us (1%)
    pallas_call x1, Pallas kernels, local(): pl.pallas_call(functools.partial(kernel, n_depth, n_tile), out_shape=pltp...  47.9 us

profile of v3, /device:TPU:7, one launch (start us, length us, event | category | flops | bytes accessed | tf_op | source)
XLA Modules:
  0.0 48.5 jit_solution(6769919289301589854)
XLA Ops:
  0.0 47.9 %shard_map.46 = f32[4,16,128]{2,1,0:T(8,128)S(1)} custom-call(f32[2,32,16,1024]{3,2,1,0:T(8,128)} %fields.1, f32[3,16]{1,0:T(4,128)} %colour.1, f32[16]{0:T(128)} %opacity.1, s32[256]{0:T(256)} %entries.1), custom_call_target="tpu_custom_call" | custom-call | tf_op jit(solution)/shard_map/pallas_call | solution.py:482
  47.9 0.6 %copy.6 = f32[4,16,128]{2,1,0:T(8,128)} copy(f32[4,16,128]{2,1,0:T(8,128)S(1)} %shard_map.46) | data formatting | bytes 65536

commit v4 on v3

--- a/solution.py
+++ b/solution.py
@@ -191,7 +191,7 @@
             part = ref.at[where]
             part[...] = jnp.zeros(part.shape, jnp.float32)
 
-    MB = 16
+    MB = 32
 
     def columns_smooth(buf, c, p):
         prev, cur, nxt = (
@@ -278,7 +278,7 @@
     def gather(table, where, axis):
         return jnp.take_along_axis(table, where, axis=axis, mode="promise_in_bounds")
 
-    G, UE = 8, 8
+    G, UE = 8, 16
 
     def stage_d(c):
         def slope(p, _):
@@ -413,7 +413,11 @@
     every(stage_b1)
 
     def in_turn(j):
-        return lax.rem(d + 1 + j, NC)
+        flips = NC - 1 - j
+        return sum(
+            bit * lax.rem(lax.div(d, bit) + lax.div(flips, bit), 2)
+            for bit in (1 << i for i in range(NC.bit_length() - 1))
+        )
 
     def middle(i, _):
         @pl.when(i < NC)
@@ -425,7 +429,7 @@
             @pl.when(i == step)
             def _():
                 for j in turns:
-                    send(3, in_turn(j))
+                    send(3, in_turn(jnp.int32(j)))
 
         @pl.when((i >= 1) & (i < NC + 1))
         def _():

time: 48.6 us -> 45.8 us (0.942)
  Pallas kernels: 47.9 us -> 45.1 us
    pallas_call x1, Pallas kernels: 47.9 us -> 45.1 us  [local(): pl.pallas_call(functools.partial(kernel, n_depth, n_tile), out_shape=pltp...]
where the time goes in v4:
time: 45.8 us; the launch traced here: 45.7 us
  Pallas kernels  45.1 us (98%)
  local copies, waits for them, and re-layouts  0.62 us (1%)
    pallas_call x1, Pallas kernels, local(): pl.pallas_call(functools.partial(kernel, n_depth, n_tile), out_shape=pltp...  45.1 us

profile of v4, /device:TPU:7, one launch (start us, length us, event | category | flops | bytes accessed | tf_op | source)
XLA Modules:
  0.0 45.7 jit_solution(5389537840314750414)
XLA Ops:
  0.0 45.1 %shard_map.46 = f32[4,16,128]{2,1,0:T(8,128)S(1)} custom-call(f32[2,32,16,1024]{3,2,1,0:T(8,128)} %fields.1, f32[3,16]{1,0:T(4,128)} %colour.1, f32[16]{0:T(128)} %opacity.1, s32[256]{0:T(256)} %entries.1), custom_call_target="tpu_custom_call" | custom-call | tf_op jit(solution)/shard_map/pallas_call | solution.py:486
  45.1 0.6 %copy.6 = f32[4,16,128]{2,1,0:T(8,128)} copy(f32[4,16,128]{2,1,0:T(8,128)S(1)} %shard_map.46) | data formatting | bytes 65536

commit v5 on v4

--- a/solution.py
+++ b/solution.py
@@ -74,7 +74,7 @@
     n_depth, n_tile,
     fields, colour, opacity, entries, out,
     F0, F1, E0, X0, S, Y1, Z1, C, PT, R, tab, idx, taps, cpal, opal, tf,
-    load_sem, table_sem, s_send, s_recv, f_send, f_recv,
+    load_sem, table_sem, met_sem, s_send, s_recv, f_send, f_recv,
 ):
     _, NZL, NXL, NYL = fields.shape
     NC = NYL // W
@@ -90,17 +90,18 @@
         )
 
     barrier = pltpu.get_barrier_semaphore()
-    beside = ((t > 0, (d, t_up)), (t < n_tile - 1, (d, t_dn)))
+    beside = (
+        (t > 0, (d, t_up)),
+        (t < n_tile - 1, (d, t_dn)),
+        (d > 0, (d_up, t)),
+        (d < n_depth - 1, (d_dn, t)),
+    )
     for present, where in beside:
 
         @pl.when(present)
         def _():
             pl.semaphore_signal(barrier, inc=1, device_id=where, device_id_type=MESH)
 
-    for step in range(1, n_depth):
-        pl.semaphore_signal(
-            barrier, inc=1, device_id=(lax.rem(d + step, n_depth), t), device_id_type=MESH
-        )
     for field in range(2):
         for c in range(NC):
             load(field, c).start()
@@ -112,13 +113,15 @@
     for copy in small:
         copy.start()
 
+    to_power = float(-0.5 * 1.5 * 2.0 / (NZL * n_depth) / np.log(2.0))
+
     def tables():
         for copy in small:
             copy.wait()
         entry = lax.broadcasted_iota(jnp.int32, (8, 16), 0)
         column = lax.broadcasted_iota(jnp.int32, (8, 16), 1)
         for j in range(4):
-            row = opal[...].reshape(1, 16) if j == 3 else cpal[j : j + 1, :]
+            row = cpal[j : j + 1, :] if j < 3 else opal[...].reshape(1, 16) * to_power
             for h in range(2):
                 picked = jnp.where(column == entry + 8 * h, jnp.broadcast_to(row, (8, 16)), 0.0)
                 tab[j, h] = jnp.broadcast_to(jnp.sum(picked, axis=1, keepdims=True), (8, W))
@@ -347,9 +350,8 @@
                 return Z1[c, p, 8 - k : 24 - k], Z1[c, p, 8 + k : 24 + k]
 
             smooth = even_sum(Z1[c, p, 8:24], pairs)
-            gate = 0.5 + 0.5 * jnp.tanh(SMOOTH_SCALE * smooth)
-            optical = (-1.5 * 2.0 / (NZL * n_depth)) * C[c, 3, p] * gate
-            kept = through * jnp.exp(optical)
+            most = C[c, 3, p]
+            kept = through * jnp.exp2(most + most * jnp.tanh(SMOOTH_SCALE * smooth))
             weight = through - kept
             return (
                 kept,
@@ -376,6 +378,28 @@
             put(PT, c)
             final_copy(c, d, c).start()
 
+    def greetings(r):
+        return (
+            (d >= 2**r, lax.rem(d + n_depth - 2**r, n_depth), 1),
+            (d < n_depth - 2**r, lax.rem(d + 2**r, n_depth), 0),
+        )
+
+    def greet(r):
+        for present, where, side in greetings(r):
+
+            @pl.when(present)
+            def _():
+                pl.semaphore_signal(
+                    met_sem.at[r, side], inc=1, device_id=(where, t), device_id_type=MESH
+                )
+
+    def met(r):
+        for present, _, side in greetings(r):
+
+            @pl.when(present)
+            def _():
+                pl.semaphore_wait(met_sem.at[r, 1 - side], 1)
+
     def every(stage, start=0):
         def step(c, _):
             stage(c)
@@ -389,16 +413,17 @@
         buf[NC + 1] = jnp.zeros_like(buf[NC + 1])
     load(0, 0).wait()
     stage_a0(0)
-    pl.semaphore_wait(
-        barrier, n_depth - 1 + (t > 0).astype(jnp.int32) + (t < n_tile - 1).astype(jnp.int32)
-    )
+    pl.semaphore_wait(barrier, sum(present.astype(jnp.int32) for present, _ in beside))
     send(0, 0)
+    greet(0)
 
     def first_field(c):
         stage_a0(c)
         send(0, c)
 
     every(first_field, 1)
+    met(0)
+    greet(1)
     load(1, 0).wait()
 
     def second_field(c):
@@ -406,6 +431,8 @@
         send(2, c)
 
     every(second_field)
+    met(1)
+    greet(2)
     tables()
     taps[1] = tap_matrices(SLOPE, True)
     S[0] = jnp.zeros_like(S[0])
@@ -446,6 +473,7 @@
     def last(j):
         stage_e(in_turn(j))
 
+    met(2)
     every(last)
 
     def wait_final(i, _):
@@ -507,6 +535,7 @@
             pltpu.VMEM(tf_index.shape, jnp.int32),
             pltpu.SemaphoreType.DMA((2, chunks)),
             pltpu.SemaphoreType.DMA((3,)),
+            pltpu.SemaphoreType.REGULAR((3, 2)),
             pltpu.SemaphoreType.DMA((4, 2, chunks)),
             pltpu.SemaphoreType.DMA((4, 2, chunks)),
             pltpu.SemaphoreType.DMA((chunks,)),

time: 45.8 us -> 45.6 us (level)
  no operation moved by 1% of the time
where the time goes in v5:
time: 45.6 us; the launch traced here: 45.5 us
  Pallas kernels  44.8 us (98%)
  local copies, waits for them, and re-layouts  0.62 us (1%)
    pallas_call x1, Pallas kernels, local(): pl.pallas_call(functools.partial(kernel, n_depth, n_tile), out_shape=pltp...  44.8 us

profile of v5, /device:TPU:7, one launch (start us, length us, event | category | flops | bytes accessed | tf_op | source)
XLA Modules:
  0.0 45.5 jit_solution(12899420755237399341)
XLA Ops:
  0.0 44.8 %shard_map.46 = f32[4,16,128]{2,1,0:T(8,128)S(1)} custom-call(f32[2,32,16,1024]{3,2,1,0:T(8,128)} %fields.1, f32[3,16]{1,0:T(4,128)} %colour.1, f32[16]{0:T(128)} %opacity.1, s32[256]{0:T(256)} %entries.1), custom_call_target="tpu_custom_call" | custom-call | tf_op jit(solution)/shard_map/pallas_call | solution.py:514
  44.9 0.6 %copy.6 = f32[4,16,128]{2,1,0:T(8,128)} copy(f32[4,16,128]{2,1,0:T(8,128)S(1)} %shard_map.46) | data formatting | bytes 65536

commit v6 on v5

--- a/solution.py
+++ b/solution.py
@@ -10,7 +10,7 @@
 
 MESH = pl.DeviceIdType.MESH
 W = 128
-THIRD = {5: (0, 1), 6: (2, 3, 4), 7: (5, 6, 7)}
+THIRD = {0: tuple(range(8))}
 
 offsets = np.arange(-4.0, 5.0)
 bell = np.exp(-(offsets**2) / 8.0)

time: 45.6 us -> 45.6 us (level)
  no operation moved by 1% of the time
where the time goes in v6:
time: 45.6 us; the launch traced here: 45.5 us
  Pallas kernels  44.9 us (98%)
  local copies, waits for them, and re-layouts  0.62 us (1%)
    pallas_call x1, Pallas kernels, local(): pl.pallas_call(functools.partial(kernel, n_depth, n_tile), out_shape=pltp...  44.9 us

profile of v6, /device:TPU:7, one launch (start us, length us, event | category | flops | bytes accessed | tf_op | source)
XLA Modules:
  0.0 45.5 jit_solution(10431164171138023599)
XLA Ops:
  0.0 44.9 %shard_map.46 = f32[4,16,128]{2,1,0:T(8,128)S(1)} custom-call(f32[2,32,16,1024]{3,2,1,0:T(8,128)} %fields.1, f32[3,16]{1,0:T(4,128)} %colour.1, f32[16]{0:T(128)} %opacity.1, s32[256]{0:T(256)} %entries.1), custom_call_target="tpu_custom_call" | custom-call | tf_op jit(solution)/shard_map/pallas_call | solution.py:514
  44.9 0.6 %copy.6 = f32[4,16,128]{2,1,0:T(8,128)} copy(f32[4,16,128]{2,1,0:T(8,128)S(1)} %shard_map.46) | data formatting | bytes 65536
